TPU v7x, 32 devices: a whole 2x2x4 slice. The times are simulated.
32 devices in a mesh: groups: 2 (over x), blk: 16 (over z, y, core).
Axes of the slice: x: 2, y: 2, z: 4, core: 2. Of those that a mesh axis runs over, the one named last changes fastest.
Arguments:
- initial_vectors: bfloat16 [192, 49152], P(('groups', 'blk')), parts along dimension 0, may hold values from -0.02734375 to 0.02734375
- final_vectors: bfloat16 [256, 49152], P(('groups', 'blk')), parts along dimension 0, may hold values from -6 to 6
- dipole: bfloat16 [3, 384, 256, 256], P(None, ('groups', 'blk')), parts along dimension 1, may hold values from -0.375 to 0.375
- block_lengths: int32 [384], P(('groups', 'blk')), parts along dimension 0, may hold values from 128 to 256, as said below
- pair_mask: int32 [192, 128], P(('groups', 'blk')), parts along dimension 0, may hold values 0 or 1
Outputs:
- strengths: float32 [192, 128], P(('groups', 'blk')), parts along dimension 0
There are 2 independent parts, one for each index of `groups`. A program takes and returns all parts, laid end to end along the dimension named above; each array names one. Nothing has to cross between parts.
Inputs may be any that keep to these rules, and one draw needn't show every extreme that they name: `block_lengths`: every block has at least half of its functions live, and the first block of each J pair is full.
All inputs are finite; a program needn't handle non-finite values. No bound on the sum of `pair_mask` on one device may be relied on, other than what follows from the above.
Results may differ from a plain program's by a relative error of at most 0.0026.
Values may be sent and summed in bfloat16 or wider, within the bound.
A program may use at most 64 MiB of HBM per device.

v0:
```python
import jax
import jax.numpy as jnp
from jax import lax
from jax.sharding import PartitionSpec as P


def on_device(initial_vectors, final_vectors, dipole, block_lengths, pair_mask):
    initial_rows, final_rows = (
        lax.all_to_all(initial_vectors, "blk", split_axis=1, concat_axis=0, tiled=True),
        lax.all_to_all(final_vectors, "blk", split_axis=1, concat_axis=0, tiled=True),
    )
    block_count = dipole.shape[1]
    block_size = dipole.shape[2]
    total_initial = initial_rows.shape[0]
    total_final = final_rows.shape[0]
    alive = jnp.arange(block_size, dtype=jnp.int32)[None, :] < block_lengths[:, None]
    alive = alive[None, :, :]
    final_blocks = final_rows.reshape(total_final, block_count, block_size)
    final_blocks = jnp.where(alive, final_blocks, jnp.zeros_like(final_blocks))
    initial_blocks = initial_rows.reshape(total_initial, block_count, block_size)
    initial_blocks = jnp.where(alive, initial_blocks, jnp.zeros_like(initial_blocks))
    half = jnp.einsum(
        "cbkl,fbl->cbkf", dipole, final_blocks, preferred_element_type=jnp.float32
    ).astype(jnp.bfloat16)
    owned = pair_mask.shape[0]
    summed = lax.psum(
        jnp.einsum("ibk,cbkf->icf", initial_blocks, half, preferred_element_type=jnp.float32), "blk"
    )
    moments = lax.dynamic_slice_in_dim(summed, lax.axis_index("blk") * owned, owned, 0)
    return pair_mask.astype(jnp.float32) * jnp.sum(moments * moments, axis=1)


def solution(mesh):
    placed = (
        P(("groups", "blk"), None),
        P(("groups", "blk"), None),
        P(None, ("groups", "blk"), None, None),
        P(("groups", "blk")),
        P(("groups", "blk"), None),
    )
    return jax.shard_map(
        on_device, mesh=mesh, in_specs=placed, out_specs=P(("groups", "blk"), None), check_vma=False
    )
```

profile of v0, /device:TPU:0, one launch (start us, length us, event | category | flops | bytes accessed | tf_op | source)
XLA Modules:
  0.0 159.4 jit_solution(11677871171764861182)
XLA Ops:
  6.5 27.7 %all_to_all.32 = bf16[6,16,3072]{2,0,1:T(8,128)(2,1)S(1)} all-to-all(bf16[6,16,3072]{2,0,1:T(8,128)(2,1)} %bitcast.20), channel_id=1, replica_groups=mesh['groups'=2,'blk'=16] {'blk'}, dimensions={1} | all-to-all | bytes 1179648 | tf_op jit(solution)/shard_map/all_to_all | solution.py:9
  34.2 3.9 %all-to-all-start.1 = ((bf16[8,16,3072]{2,0,1:T(8,128)(2,1)}), bf16[8,16,3072]{2,0,1:T(8,128)(2,1)S(1)}, u32[]{:S(2)}, u32[]{:S(2)}) async-start(bf16[8,16,3072]{2,0,1:T(8,128)(2,1)} %bitcast.21), calls=%async_computation.1 | async-start | bytes 1572864 | tf_op jit(solution)/shard_map/all_to_all | solution.py:10
  38.1 0.0 all-reduce.2.cloned.1.call-start
  38.2 0.7 iota_compare_fusion
  38.9 0.6 reshape.32
  39.5 0.9 broadcast_select_fusion
  40.5 16.3 %all-to-all-done.1 = bf16[8,16,3072]{2,0,1:T(8,128)(2,1)S(1)} async-done(((bf16[8,16,3072]{2,0,1:T(8,128)(2,1)}), bf16[8,16,3072]{2,0,1:T(8,128)(2,1)S(1)}, u32[]{:S(2)}, u32[]{:S(2)}) %all-to-all-start.1) | async-done | bytes 786464 | tf_op jit(solution)/shard_map/all_to_all | solution.py:10
  56.8 0.5 reshape.33
  57.3 0.0 copy-start
  57.4 0.1 select_bitcast_fusion
  57.4 5.1 %fusion.5 = f32[96,3,128]{2,0,1:T(8,128)} fusion(bf16[3,12,256,256]{3,2,1,0:T(8,128)(2,1)} %param.7, bf16[128,12,256,1]{2,1,0,3:T(8,128)(2,1)S(1)} %select_bitcast_fusion, bf16[96,12,256]{2,1,0:T(8,128)(2,1)} %broadcast_select_fusion), kind=kOutput, calls=%fused_computation.4 | convolution fusion | flops 831651840 | bytes 6242304 | tf_op jit(solution)/shard_map/ibk,cbkf->icf/dot_general | solution.py:27
  62.6 0.0 all-reduce.2.cloned.1.call-update
  62.6 88.6 %all-reduce.2.cloned.1.call-done = f32[96,3,128]{2,0,1:T(8,128)} async-done(((f32[96,3,128]{2,0,1:T(8,128)}), f32[96,3,128]{2,0,1:T(8,128)}) %all-reduce.2.cloned.1.call-update) | async-done | bytes 147472 | tf_op jit(solution)/shard_map/psum | solution.py:26
  151.2 0.7 multiply_reduce_fusion
  151.9 0.0 copy-done
  152.0 0.6 convert_multiply_fusion
Async XLA Ops:
  34.2 22.6 %all-to-all-start.1 = ((bf16[8,16,3072]{2,0,1:T(8,128)(2,1)}), bf16[8,16,3072]{2,0,1:T(8,128)(2,1)S(1)}, u32[]{:S(2)}, u32[]{:S(2)}) async-start(bf16[8,16,3072]{2,0,1:T(8,128)(2,1)} %bitcast.21), calls=%async_computation.1 | async-start | bytes 1572864 | tf_op jit(solution)/shard_map/all_to_all | solution.py:10
  38.1 113.1 %all-reduce.2.cloned.1.call-start = ((), (), s32[]{:S(2)}) async-start(), calls=%async_computation.2 | async-start | bytes 294912 | tf_op jit(solution)/shard_map/psum | solution.py:26
  57.3 94.6 %copy-start = (s32[6,128]{1,0:T(8,128)S(1)}, s32[6,128]{1,0:T(8,128)}, u32[]{:S(2)}) copy-start(s32[6,128]{1,0:T(8,128)} %param.9) | copy-start | bytes 9220
Sparse Core Ops, SparseCore 0:
  62.7 88.4 all-reduce.1
where the time goes:
time: 160 us; the launch traced here: 159 us
  waiting for transfers between devices  105 us (66%)
  blocking collectives  27.7 us (17%)
  between operations  13.4 us (8%)
  matrix products  5.13 us (3%)
  starting transfers between devices  3.95 us (2%)
  other arithmetic  3.09 us (2%)
    psum x1, waiting for transfers between devices, on_device(): lax.psum(jnp.einsum('ibk,cbkf->icf', initial_blocks, half, preferred_elem...  88.6 us
    all_to_all x1, blocking collectives, on_device(): lax.all_to_all(initial_vectors, 'blk', split_axis=1, concat_axis=0, tiled...  27.7 us
    all_to_all x1, waiting for transfers between devices, on_device(): lax.all_to_all(final_vectors, 'blk', split_axis=1, concat_axis=0, tiled=T...  16.3 us
    dot_general x1, matrix products, on_device(): jnp.einsum('ibk,cbkf->icf', initial_blocks, half, preferred_element_type=...  5.13 us
    all_to_all x1, starting transfers between devices, on_device(): lax.all_to_all(final_vectors, 'blk', split_axis=1, concat_axis=0, tiled=T...  3.91 us
  transfers between devices with their start and end apart: 2, of which 2 were waited for; matrix products, arithmetic and copies ran while one was open for 1% of the time, Pallas kernels for 0%

commit v1 on v0

v1 whole, which is shorter than its diff:
```python
import functools

import jax
import jax.numpy as jnp
from jax import lax
from jax.experimental import pallas as pl
from jax.experimental.pallas import tpu as pltpu
from jax.sharding import PartitionSpec as P

MESH = pl.DeviceIdType.MESH


def kernel(
    n, chunks,
    initial, final, dipole, lengths, mask, out,
    final_in, initial_in, tiles, partial, arrived,
    tile_sem, send_sem, final_sem, initial_sem, moment_send, moment_recv,
):
    me = lax.axis_index("blk")
    components, blocks, size, _ = dipole.shape
    per_chunk = blocks // chunks
    width = per_chunk * size
    owned, owned_final = initial.shape[0], final.shape[0]
    padded = partial.shape[1]

    tile_copy = pltpu.make_async_copy(dipole, tiles, tile_sem)
    tile_copy.start()

    def columns(owner, chunk):
        return pl.ds(pl.multiple_of(owner * (blocks * size) + chunk * width, size), width)

    for chunk in range(chunks):
        pltpu.make_async_copy(
            final.at[:, columns(me, chunk)], final_in.at[chunk, me], final_sem.at[chunk]
        ).start()
        pltpu.make_async_copy(
            initial.at[:, columns(me, chunk)], initial_in.at[chunk, me], initial_sem.at[chunk]
        ).start()

    barrier = pltpu.get_barrier_semaphore()

    def greet(step, carry):
        pl.semaphore_signal(
            barrier, inc=1, device_id={"blk": lax.rem(me + step, n)}, device_id_type=MESH
        )
        return carry

    lax.fori_loop(1, n, greet, 0)
    pl.semaphore_wait(barrier, n - 1)

    for chunk in range(chunks):

        def send(step, carry):
            peer = lax.rem(me + step, n)
            pltpu.make_async_remote_copy(
                final.at[:, columns(peer, chunk)], final_in.at[chunk, me],
                send_sem.at[0, chunk], final_sem.at[chunk],
                device_id={"blk": peer}, device_id_type=MESH,
            ).start()
            pltpu.make_async_remote_copy(
                initial.at[:, columns(peer, chunk)], initial_in.at[chunk, me],
                send_sem.at[1, chunk], initial_sem.at[chunk],
                device_id={"blk": peer}, device_id_type=MESH,
            ).start()
            return carry

        lax.fori_loop(1, n, send, 0)

    tile_copy.wait()
    total = [jnp.zeros((n * padded, n * owned_final), jnp.float32)] * components
    for chunk in range(chunks):
        pltpu.make_async_copy(final_in.at[chunk], final_in.at[chunk], final_sem.at[chunk]).wait()
        pltpu.make_async_copy(initial_in.at[chunk], initial_in.at[chunk], initial_sem.at[chunk]).wait()
        for j in range(per_chunk):
            block = chunk * per_chunk + j
            alive = lax.broadcasted_iota(jnp.int32, (1, 1, size), 2) < lengths[block]
            finals = final_in[chunk, :, :, j * size : (j + 1) * size].astype(jnp.float32)
            finals = jnp.where(alive, finals, 0.0).reshape(n * owned_final, size).astype(jnp.bfloat16)
            initials = initial_in[chunk, :, :, j * size : (j + 1) * size].astype(jnp.float32)
            initials = jnp.where(alive, initials, 0.0)
            if padded > owned:
                initials = jnp.concatenate(
                    [initials, jnp.zeros((n, padded - owned, size), jnp.float32)], axis=1
                )
            initials = initials.reshape(n * padded, size).astype(jnp.bfloat16)
            half = lax.dot_general(
                tiles[:, block].reshape(components * size, size), finals,
                (((1,), (1,)), ((), ())), preferred_element_type=jnp.float32,
            ).astype(jnp.bfloat16)
            for c in range(components):
                total[c] = total[c] + jnp.dot(
                    initials, half[c * size : (c + 1) * size], preferred_element_type=jnp.float32
                )
    finals_all = n * owned_final
    for c in range(components):
        partial[:, :, c * finals_all : (c + 1) * finals_all] = total[c].reshape(n, padded, finals_all)

    def spread(step, carry):
        peer = lax.rem(me + step, n)
        pltpu.make_async_remote_copy(
            partial.at[peer], arrived.at[me], moment_send, moment_recv,
            device_id={"blk": peer}, device_id_type=MESH,
        ).start()
        return carry

    lax.fori_loop(1, n, spread, 0)
    pltpu.make_async_copy(partial.at[me], arrived.at[me], moment_recv).start()
    pltpu.make_async_copy(arrived, arrived, moment_recv).wait()
    moments = jnp.sum(arrived[...], axis=0)
    squares = moments * moments
    strength = squares[:, :finals_all]
    for c in range(1, components):
        strength = strength + squares[:, c * finals_all : (c + 1) * finals_all]
    out[...] = mask[...].astype(jnp.float32) * strength[:owned]

    for chunk in range(chunks):
        pltpu.make_async_copy(
            final_in.at[chunk, pl.ds(0, n - 1)], final_in.at[chunk, pl.ds(0, n - 1)], send_sem.at[0, chunk]
        ).wait()
        pltpu.make_async_copy(
            initial_in.at[chunk, pl.ds(0, n - 1)], initial_in.at[chunk, pl.ds(0, n - 1)], send_sem.at[1, chunk]
        ).wait()
    pltpu.make_async_copy(
        partial.at[pl.ds(0, n - 1)], partial.at[pl.ds(0, n - 1)], moment_send
    ).wait()


def on_device(n, initial_vectors, final_vectors, dipole, block_lengths, pair_mask):
    components, blocks, size, _ = dipole.shape
    owned, owned_final = initial_vectors.shape[0], final_vectors.shape[0]
    chunks = 4
    width = blocks // chunks * size
    padded = -(-owned // 8) * 8
    return pl.pallas_call(
        functools.partial(kernel, n, chunks),
        out_shape=jax.ShapeDtypeStruct(pair_mask.shape, jnp.float32),
        in_specs=[
            pl.BlockSpec(memory_space=pl.ANY),
            pl.BlockSpec(memory_space=pl.ANY),
            pl.BlockSpec(memory_space=pl.ANY),
            pl.BlockSpec(memory_space=pltpu.SMEM),
            pl.BlockSpec(memory_space=pltpu.VMEM),
        ],
        out_specs=pl.BlockSpec(memory_space=pltpu.VMEM),
        scratch_shapes=[
            pltpu.VMEM((chunks, n, owned_final, width), jnp.bfloat16),
            pltpu.VMEM((chunks, n, owned, width), jnp.bfloat16),
            pltpu.VMEM(dipole.shape, jnp.bfloat16),
            pltpu.VMEM((n, padded, components * n * owned_final), jnp.float32),
            pltpu.VMEM((n, padded, components * n * owned_final), jnp.float32),
            pltpu.SemaphoreType.DMA,
            pltpu.SemaphoreType.DMA((2, chunks)),
            pltpu.SemaphoreType.DMA((chunks,)),
            pltpu.SemaphoreType.DMA((chunks,)),
            pltpu.SemaphoreType.DMA,
            pltpu.SemaphoreType.DMA,
        ],
        compiler_params=pltpu.CompilerParams(
            collective_id=0, has_side_effects=True, vmem_limit_bytes=56 * 1024 * 1024
        ),
        cost_estimate=pl.CostEstimate(
            flops=2 * components * blocks * size * n * owned_final * (size + n * padded),
            bytes_accessed=2 * components * blocks * size * size + 4 * n * width * chunks * owned_final,
            transcendentals=0,
        ),
    )(initial_vectors, final_vectors, dipole, block_lengths, pair_mask)


def solution(mesh):
    placed = (
        P(("groups", "blk"), None),
        P(("groups", "blk"), None),
        P(None, ("groups", "blk"), None, None),
        P(("groups", "blk")),
        P(("groups", "blk"), None),
    )
    return jax.shard_map(
        functools.partial(on_device, mesh.shape["blk"]),
        mesh=mesh, in_specs=placed, out_specs=P(("groups", "blk"), None), check_vma=False,
    )
```

time: 160 us -> 50.6 us (0.32)
  waiting for transfers between devices: 105 us -> 0 us
  Pallas kernels: 0 us -> 49.1 us
  blocking collectives: 27.7 us -> 0 us
  between operations: 13.4 us -> 0.01 us
  matrix products: 5.13 us -> 0 us
  starting transfers between devices: 3.95 us -> 0 us
  other arithmetic: 3.09 us -> 0 us
    psum x1 -> x0, waiting for transfers between devices: 88.6 us -> none  [on_device(): lax.psum(jnp.einsum('ibk,cbkf->icf', initial_blocks, half, preferred_elem...]
    pallas_call x0 -> x1, Pallas kernels: none -> 49.1 us  [on_device(): pl.pallas_call(functools.partial(kernel, n, chunks), out_shape=jax.ShapeD...]
    all_to_all x1 -> x0, blocking collectives: 27.7 us -> none  [on_device(): lax.all_to_all(initial_vectors, 'blk', split_axis=1, concat_axis=0, tiled...]
    all_to_all x1 -> x0, waiting for transfers between devices: 16.3 us -> none  [on_device(): lax.all_to_all(final_vectors, 'blk', split_axis=1, concat_axis=0, tiled=T...]
    dot_general x1 -> x0, matrix products: 5.13 us -> none  [on_device(): jnp.einsum('ibk,cbkf->icf', initial_blocks, half, preferred_element_type=...]
    all_to_all x1 -> x0, starting transfers between devices: 3.91 us -> none  [on_device(): lax.all_to_all(final_vectors, 'blk', split_axis=1, concat_axis=0, tiled=T...]
  transfers between devices with their start and end apart: 2 -> 0, of which waited for: 2 -> 0; matrix products, arithmetic and copies ran while one was open for 1% -> 0% of each run, Pallas kernels for 0% -> 0%
where the time goes in v1:
time: 50.6 us; the launch traced here: 50.4 us
  Pallas kernels  49.1 us (97%)
  local copies, waits for them, and re-layouts  1.28 us (3%)
    pallas_call x1, Pallas kernels, on_device(): pl.pallas_call(functools.partial(kernel, n, chunks), out_shape=jax.ShapeD...  49.1 us
    unnamed x1, local copies, waits for them, and re-layouts  1.28 us

profile of v1, /device:TPU:0, one launch (start us, length us, event | category | flops | bytes accessed | tf_op | source)
XLA Modules:
  0.0 50.4 jit_solution(4801916534148171017)
XLA Ops:
  0.0 49.1 %shard_map.55 = f32[6,128]{1,0:T(8,128)} custom-call(bf16[6,49152]{1,0:T(8,128)(2,1)} %initial.1, bf16[8,49152]{1,0:T(8,128)(2,1)} %final.1, bf16[3,12,256,256]{3,2,1,0:T(8,128)(2,1)} %dipole.1, s32[12]{0:T(128)} %lengths.1, s32[6,128]{1,0:T(8,128)} %mask.1), custom_call_target="tpu_custom_call" | custom-call | flops 905969664 | bytes 6291456 | tf_op jit(solution)/shard_map/pallas_call | solution.py:134
  49.1 1.3 %copy.7 = f32[6,128]{1,0:T(8,128)} copy(f32[6,128]{1,0:T(8,128)} %shard_map.55) | data formatting | bytes 6144

commit v2 on v1

--- a/solution.py
+++ b/solution.py
@@ -13,8 +13,8 @@
 def kernel(
     n, chunks,
     initial, final, dipole, lengths, mask, out,
-    final_in, initial_in, tiles, partial, arrived,
-    tile_sem, send_sem, final_sem, initial_sem, moment_send, moment_recv,
+    staged, packed, final_in, initial_in, tiles, partial, arrived,
+    stage_sem, tile_sem, send_sem, final_sem, initial_sem, moment_send, moment_recv,
 ):
     me = lax.axis_index("blk")
     components, blocks, size, _ = dipole.shape
@@ -22,7 +22,11 @@
     width = per_chunk * size
     owned, owned_final = initial.shape[0], final.shape[0]
     padded = partial.shape[1]
-
+    spare = padded - owned
+    full = chunks - 1
+
+    stage_copy = pltpu.make_async_copy(initial, staged, stage_sem)
+    stage_copy.start()
     tile_copy = pltpu.make_async_copy(dipole, tiles, tile_sem)
     tile_copy.start()
 
@@ -32,9 +36,6 @@
     for chunk in range(chunks):
         pltpu.make_async_copy(
             final.at[:, columns(me, chunk)], final_in.at[chunk, me], final_sem.at[chunk]
-        ).start()
-        pltpu.make_async_copy(
-            initial.at[:, columns(me, chunk)], initial_in.at[chunk, me], initial_sem.at[chunk]
         ).start()
 
     barrier = pltpu.get_barrier_semaphore()
@@ -46,6 +47,26 @@
         return carry
 
     lax.fori_loop(1, n, greet, 0)
+
+    stage_copy.wait()
+
+    def pack(owner, carry):
+        start = pl.multiple_of(owner * (blocks * size), blocks * size)
+        rows = staged[:, pl.ds(start, blocks * size)].astype(jnp.float32)
+        last = rows[:, full * width :]
+        for chunk in range(full):
+            packed[owner, chunk] = jnp.concatenate(
+                [rows[:, chunk * width : (chunk + 1) * width]]
+                + [last[chunk + e * full : chunk + e * full + 1] for e in range(spare)],
+                axis=0,
+            ).astype(jnp.bfloat16)
+        return carry
+
+    lax.fori_loop(0, n, pack, 0)
+    for chunk in range(full):
+        pltpu.make_async_copy(
+            packed.at[me, chunk], initial_in.at[chunk, me], initial_sem.at[chunk]
+        ).start()
     pl.semaphore_wait(barrier, n - 1)
 
     for chunk in range(chunks):
@@ -57,11 +78,12 @@
                 send_sem.at[0, chunk], final_sem.at[chunk],
                 device_id={"blk": peer}, device_id_type=MESH,
             ).start()
-            pltpu.make_async_remote_copy(
-                initial.at[:, columns(peer, chunk)], initial_in.at[chunk, me],
-                send_sem.at[1, chunk], initial_sem.at[chunk],
-                device_id={"blk": peer}, device_id_type=MESH,
-            ).start()
+            if chunk < full:
+                pltpu.make_async_remote_copy(
+                    packed.at[peer, chunk], initial_in.at[chunk, me],
+                    send_sem.at[1, chunk], initial_sem.at[chunk],
+                    device_id={"blk": peer}, device_id_type=MESH,
+                ).start()
             return carry
 
         lax.fori_loop(1, n, send, 0)
@@ -70,18 +92,26 @@
     total = [jnp.zeros((n * padded, n * owned_final), jnp.float32)] * components
     for chunk in range(chunks):
         pltpu.make_async_copy(final_in.at[chunk], final_in.at[chunk], final_sem.at[chunk]).wait()
-        pltpu.make_async_copy(initial_in.at[chunk], initial_in.at[chunk], initial_sem.at[chunk]).wait()
+        if chunk < full:
+            pltpu.make_async_copy(initial_in.at[chunk], initial_in.at[chunk], initial_sem.at[chunk]).wait()
         for j in range(per_chunk):
             block = chunk * per_chunk + j
             alive = lax.broadcasted_iota(jnp.int32, (1, 1, size), 2) < lengths[block]
             finals = final_in[chunk, :, :, j * size : (j + 1) * size].astype(jnp.float32)
             finals = jnp.where(alive, finals, 0.0).reshape(n * owned_final, size).astype(jnp.bfloat16)
-            initials = initial_in[chunk, :, :, j * size : (j + 1) * size].astype(jnp.float32)
+            place = slice(j * size, (j + 1) * size)
+            if chunk < full:
+                initials = initial_in[chunk, :, :, place].astype(jnp.float32)
+            else:
+                carried = [
+                    initial_in[g, :, owned:, place].astype(jnp.float32) for g in range(full)
+                ]
+                initials = jnp.concatenate(
+                    [carried[r % full][:, r // full : r // full + 1] for r in range(owned)]
+                    + [jnp.zeros((n, spare, size), jnp.float32)],
+                    axis=1,
+                )
             initials = jnp.where(alive, initials, 0.0)
-            if padded > owned:
-                initials = jnp.concatenate(
-                    [initials, jnp.zeros((n, padded - owned, size), jnp.float32)], axis=1
-                )
             initials = initials.reshape(n * padded, size).astype(jnp.bfloat16)
             half = lax.dot_general(
                 tiles[:, block].reshape(components * size, size), finals,
@@ -117,9 +147,10 @@
         pltpu.make_async_copy(
             final_in.at[chunk, pl.ds(0, n - 1)], final_in.at[chunk, pl.ds(0, n - 1)], send_sem.at[0, chunk]
         ).wait()
-        pltpu.make_async_copy(
-            initial_in.at[chunk, pl.ds(0, n - 1)], initial_in.at[chunk, pl.ds(0, n - 1)], send_sem.at[1, chunk]
-        ).wait()
+        if chunk < full:
+            pltpu.make_async_copy(
+                initial_in.at[chunk, pl.ds(0, n - 1)], initial_in.at[chunk, pl.ds(0, n - 1)], send_sem.at[1, chunk]
+            ).wait()
     pltpu.make_async_copy(
         partial.at[pl.ds(0, n - 1)], partial.at[pl.ds(0, n - 1)], moment_send
     ).wait()
@@ -128,9 +159,11 @@
 def on_device(n, initial_vectors, final_vectors, dipole, block_lengths, pair_mask):
     components, blocks, size, _ = dipole.shape
     owned, owned_final = initial_vectors.shape[0], final_vectors.shape[0]
-    chunks = 4
+    padded = (owned // 8 + 1) * 8
+    full = -(-owned // (padded - owned))
+    chunks = full + 1
+    assert blocks % chunks == 0 and full * (padded - owned) == owned
     width = blocks // chunks * size
-    padded = -(-owned // 8) * 8
     return pl.pallas_call(
         functools.partial(kernel, n, chunks),
         out_shape=jax.ShapeDtypeStruct(pair_mask.shape, jnp.float32),
@@ -143,11 +176,14 @@
         ],
         out_specs=pl.BlockSpec(memory_space=pltpu.VMEM),
         scratch_shapes=[
+            pltpu.VMEM(initial_vectors.shape, jnp.bfloat16),
+            pltpu.VMEM((n, full, padded, width), jnp.bfloat16),
             pltpu.VMEM((chunks, n, owned_final, width), jnp.bfloat16),
-            pltpu.VMEM((chunks, n, owned, width), jnp.bfloat16),
+            pltpu.VMEM((full, n, padded, width), jnp.bfloat16),
             pltpu.VMEM(dipole.shape, jnp.bfloat16),
             pltpu.VMEM((n, padded, components * n * owned_final), jnp.float32),
             pltpu.VMEM((n, padded, components * n * owned_final), jnp.float32),
+            pltpu.SemaphoreType.DMA,
             pltpu.SemaphoreType.DMA,
             pltpu.SemaphoreType.DMA((2, chunks)),
             pltpu.SemaphoreType.DMA((chunks,)),

time: 50.6 us -> 46.6 us (0.921)
  Pallas kernels: 49.1 us -> 45.1 us
    pallas_call x1, Pallas kernels: 49.1 us -> 45.1 us  [on_device(): pl.pallas_call(functools.partial(kernel, n, chunks), out_shape=jax.ShapeD...]
where the time goes in v2:
time: 46.6 us; the launch traced here: 46.4 us
  Pallas kernels  45.1 us (97%)
  local copies, waits for them, and re-layouts  1.28 us (3%)
    pallas_call x1, Pallas kernels, on_device(): pl.pallas_call(functools.partial(kernel, n, chunks), out_shape=jax.ShapeD...  45.1 us
    unnamed x1, local copies, waits for them, and re-layouts  1.28 us

profile of v2, /device:TPU:0, one launch (start us, length us, event | category | flops | bytes accessed | tf_op | source)
XLA Modules:
  0.0 46.4 jit_solution(5094142760969727708)
XLA Ops:
  0.0 45.1 %shard_map.55 = f32[6,128]{1,0:T(8,128)} custom-call(bf16[6,49152]{1,0:T(8,128)(2,1)} %initial.1, bf16[8,49152]{1,0:T(8,128)(2,1)} %final.1, bf16[3,12,256,256]{3,2,1,0:T(8,128)(2,1)} %dipole.1, s32[12]{0:T(128)} %lengths.1, s32[6,128]{1,0:T(8,128)} %mask.1), custom_call_target="tpu_custom_call" | custom-call | flops 905969664 | bytes 6291456 | tf_op jit(solution)/shard_map/pallas_call | solution.py:167
  45.2 1.3 %copy.7 = f32[6,128]{1,0:T(8,128)} copy(f32[6,128]{1,0:T(8,128)} %shard_map.55) | data formatting | bytes 6144

commit v3 on v2

--- a/solution.py
+++ b/solution.py
@@ -14,14 +14,14 @@
     n, chunks,
     initial, final, dipole, lengths, mask, out,
     staged, packed, final_in, initial_in, tiles, partial, arrived,
-    stage_sem, tile_sem, send_sem, final_sem, initial_sem, moment_send, moment_recv,
+    stage_sem, tile_sem, send_sem, final_sem, initial_sem, moment_send, moment_recv, passed,
 ):
     me = lax.axis_index("blk")
     components, blocks, size, _ = dipole.shape
     per_chunk = blocks // chunks
     width = per_chunk * size
     owned, owned_final = initial.shape[0], final.shape[0]
-    padded = partial.shape[1]
+    padded = packed.shape[2]
     spare = padded - owned
     full = chunks - 1
 
@@ -40,10 +40,19 @@
 
     barrier = pltpu.get_barrier_semaphore()
 
+    per_quarter = n // 4
+    quarter, local = me // per_quarter, lax.rem(me, per_quarter)
+
+    def distance(peer):
+        return jnp.abs(peer // per_quarter - quarter)
+
     def greet(step, carry):
-        pl.semaphore_signal(
-            barrier, inc=1, device_id={"blk": lax.rem(me + step, n)}, device_id_type=MESH
-        )
+        peer = lax.rem(me + step, n)
+
+        @pl.when(distance(peer) <= 1)
+        def _():
+            pl.semaphore_signal(barrier, inc=1, device_id={"blk": peer}, device_id_type=MESH)
+
         return carry
 
     lax.fori_loop(1, n, greet, 0)
@@ -67,12 +76,31 @@
         pltpu.make_async_copy(
             packed.at[me, chunk], initial_in.at[chunk, me], initial_sem.at[chunk]
         ).start()
-    pl.semaphore_wait(barrier, n - 1)
-
-    for chunk in range(chunks):
-
-        def send(step, carry):
-            peer = lax.rem(me + step, n)
+    inner = (quarter > 0).astype(jnp.int32) + (quarter < 3).astype(jnp.int32)
+    pl.semaphore_wait(barrier, per_quarter * (1 + inner) - 1)
+
+    def pass_on(hops):
+        for side in (1, -1):
+            target = quarter + side
+            behind = quarter - side * (hops - 1)
+
+            @pl.when((target >= 0) & (target <= 3) & (behind >= 0) & (behind <= 3))
+            def _():
+                pl.semaphore_signal(
+                    passed.at[hops - 2, (1 - side) // 2], inc=1,
+                    device_id={"blk": target * per_quarter + local}, device_id_type=MESH,
+                )
+
+        for side in (1, -1):
+            source = quarter - side * hops
+
+            @pl.when((source >= 0) & (source <= 3))
+            def _():
+                pl.semaphore_wait(passed.at[hops - 2, (1 - side) // 2], 1)
+
+    for chunk in range(chunks):
+
+        def send_to(peer):
             pltpu.make_async_remote_copy(
                 final.at[:, columns(peer, chunk)], final_in.at[chunk, me],
                 send_sem.at[0, chunk], final_sem.at[chunk],
@@ -84,11 +112,34 @@
                     send_sem.at[1, chunk], initial_sem.at[chunk],
                     device_id={"blk": peer}, device_id_type=MESH,
                 ).start()
+
+        def send(step, carry):
+            send_to(lax.rem(me + step, n))
             return carry
 
-        lax.fori_loop(1, n, send, 0)
+        def send_within(low, high):
+            def step_to(step, carry):
+                peer = lax.rem(me + step, n)
+
+                @pl.when((distance(peer) >= low) & (distance(peer) <= high))
+                def _():
+                    send_to(peer)
+
+                return carry
+
+            lax.fori_loop(1, n, step_to, 0)
+
+        if chunk == 0:
+            send_within(0, 1)
+            pass_on(2)
+            send_within(2, 2)
+            pass_on(3)
+            send_within(3, 3)
+        else:
+            lax.fori_loop(1, n, send, 0)
 
     tile_copy.wait()
+    finals_all = n * owned_final
     total = [jnp.zeros((n * padded, n * owned_final), jnp.float32)] * components
     for chunk in range(chunks):
         pltpu.make_async_copy(final_in.at[chunk], final_in.at[chunk], final_sem.at[chunk]).wait()
@@ -121,9 +172,14 @@
                 total[c] = total[c] + jnp.dot(
                     initials, half[c * size : (c + 1) * size], preferred_element_type=jnp.float32
                 )
-    finals_all = n * owned_final
+    lanes = partial.shape[2]
+    pieces = finals_all // lanes
     for c in range(components):
-        partial[:, :, c * finals_all : (c + 1) * finals_all] = total[c].reshape(n, padded, finals_all)
+        for p in range(pieces):
+            row = (c * pieces + p) * owned
+            partial[:, row : row + owned, :] = total[c][:, p * lanes : (p + 1) * lanes].reshape(
+                n, padded, lanes
+            )[:, :owned]
 
     def spread(step, carry):
         peer = lax.rem(me + step, n)
@@ -137,11 +193,15 @@
     pltpu.make_async_copy(partial.at[me], arrived.at[me], moment_recv).start()
     pltpu.make_async_copy(arrived, arrived, moment_recv).wait()
     moments = jnp.sum(arrived[...], axis=0)
-    squares = moments * moments
-    strength = squares[:, :finals_all]
-    for c in range(1, components):
-        strength = strength + squares[:, c * finals_all : (c + 1) * finals_all]
-    out[...] = mask[...].astype(jnp.float32) * strength[:owned]
+    strengths = []
+    for p in range(pieces):
+        strength = jnp.zeros((owned, lanes), jnp.float32)
+        for c in range(components):
+            row = (c * pieces + p) * owned
+            strength = strength + moments[row : row + owned] * moments[row : row + owned]
+        strengths.append(strength)
+    strength = jnp.concatenate(strengths, axis=1)
+    out[...] = mask[...].astype(jnp.float32) * strength
 
     for chunk in range(chunks):
         pltpu.make_async_copy(
@@ -181,8 +241,8 @@
             pltpu.VMEM((chunks, n, owned_final, width), jnp.bfloat16),
             pltpu.VMEM((full, n, padded, width), jnp.bfloat16),
             pltpu.VMEM(dipole.shape, jnp.bfloat16),
-            pltpu.VMEM((n, padded, components * n * owned_final), jnp.float32),
-            pltpu.VMEM((n, padded, components * n * owned_final), jnp.float32),
+            pltpu.VMEM((n, components * (n * owned_final // 128) * owned, 128), jnp.float32),
+            pltpu.VMEM((n, components * (n * owned_final // 128) * owned, 128), jnp.float32),
             pltpu.SemaphoreType.DMA,
             pltpu.SemaphoreType.DMA,
             pltpu.SemaphoreType.DMA((2, chunks)),
@@ -190,6 +250,7 @@
             pltpu.SemaphoreType.DMA((chunks,)),
             pltpu.SemaphoreType.DMA,
             pltpu.SemaphoreType.DMA,
+            pltpu.SemaphoreType.REGULAR((2, 2)),
         ],
         compiler_params=pltpu.CompilerParams(
             collective_id=0, has_side_effects=True, vmem_limit_bytes=56 * 1024 * 1024

time: 46.6 us -> 45.8 us (0.983)
  Pallas kernels: 45.1 us -> 44.2 us
    pallas_call x1, Pallas kernels: 45.1 us -> 44.2 us  [on_device(): pl.pallas_call(functools.partial(kernel, n, chunks), out_shape=jax.ShapeD...]
where the time goes in v3:
time: 45.8 us; the launch traced here: 45.5 us
  Pallas kernels  44.2 us (97%)
  local copies, waits for them, and re-layouts  1.28 us (3%)
    pallas_call x1, Pallas kernels, on_device(): pl.pallas_call(functools.partial(kernel, n, chunks), out_shape=jax.ShapeD...  44.2 us
    unnamed x1, local copies, waits for them, and re-layouts  1.28 us

profile of v3, /device:TPU:0, one launch (start us, length us, event | category | flops | bytes accessed | tf_op | source)
XLA Modules:
  0.0 45.5 jit_solution(13595300266802190726)
XLA Ops:
  0.0 44.2 %shard_map.55 = f32[6,128]{1,0:T(8,128)} custom-call(bf16[6,49152]{1,0:T(8,128)(2,1)} %initial.1, bf16[8,49152]{1,0:T(8,128)(2,1)} %final.1, bf16[3,12,256,256]{3,2,1,0:T(8,128)(2,1)} %dipole.1, s32[12]{0:T(128)} %lengths.1, s32[6,128]{1,0:T(8,128)} %mask.1), custom_call_target="tpu_custom_call" | custom-call | flops 905969664 | bytes 6291456 | tf_op jit(solution)/shard_map/pallas_call | solution.py:227
  44.2 1.3 %copy.7 = f32[6,128]{1,0:T(8,128)} copy(f32[6,128]{1,0:T(8,128)} %shard_map.55) | data formatting | bytes 6144

commit v4 on v3

--- a/solution.py
+++ b/solution.py
@@ -138,32 +138,37 @@
         else:
             lax.fori_loop(1, n, send, 0)
 
+    def live_initials(chunk, j):
+        alive = lax.broadcasted_iota(jnp.int32, (1, 1, size), 2) < lengths[chunk * per_chunk + j]
+        place = slice(j * size, (j + 1) * size)
+        if chunk < full:
+            initials = initial_in[chunk, :, :, place].astype(jnp.float32)
+        else:
+            carried = [
+                initial_in[g, :, owned:, place].astype(jnp.float32) for g in range(full)
+            ]
+            initials = jnp.concatenate(
+                [carried[r % full][:, r // full : r // full + 1] for r in range(owned)]
+                + [jnp.zeros((n, spare, size), jnp.float32)],
+                axis=1,
+            )
+        initials = jnp.where(alive, initials, 0.0)
+        return initials.reshape(n * padded, size).astype(jnp.bfloat16)
+
     tile_copy.wait()
     finals_all = n * owned_final
     total = [jnp.zeros((n * padded, n * owned_final), jnp.float32)] * components
     for chunk in range(chunks):
-        pltpu.make_async_copy(final_in.at[chunk], final_in.at[chunk], final_sem.at[chunk]).wait()
         if chunk < full:
             pltpu.make_async_copy(initial_in.at[chunk], initial_in.at[chunk], initial_sem.at[chunk]).wait()
+        states = [live_initials(chunk, j) for j in range(per_chunk)]
+        pltpu.make_async_copy(final_in.at[chunk], final_in.at[chunk], final_sem.at[chunk]).wait()
         for j in range(per_chunk):
             block = chunk * per_chunk + j
             alive = lax.broadcasted_iota(jnp.int32, (1, 1, size), 2) < lengths[block]
             finals = final_in[chunk, :, :, j * size : (j + 1) * size].astype(jnp.float32)
             finals = jnp.where(alive, finals, 0.0).reshape(n * owned_final, size).astype(jnp.bfloat16)
-            place = slice(j * size, (j + 1) * size)
-            if chunk < full:
-                initials = initial_in[chunk, :, :, place].astype(jnp.float32)
-            else:
-                carried = [
-                    initial_in[g, :, owned:, place].astype(jnp.float32) for g in range(full)
-                ]
-                initials = jnp.concatenate(
-                    [carried[r % full][:, r // full : r // full + 1] for r in range(owned)]
-                    + [jnp.zeros((n, spare, size), jnp.float32)],
-                    axis=1,
-                )
-            initials = jnp.where(alive, initials, 0.0)
-            initials = initials.reshape(n * padded, size).astype(jnp.bfloat16)
+            initials = states[j]
             half = lax.dot_general(
                 tiles[:, block].reshape(components * size, size), finals,
                 (((1,), (1,)), ((), ())), preferred_element_type=jnp.float32,
@@ -182,7 +187,7 @@
             )[:, :owned]
 
     def spread(step, carry):
-        peer = lax.rem(me + step, n)
+        peer = lax.rem(me + 1 + lax.rem(step - 1 + n // 4, n - 1), n)
         pltpu.make_async_remote_copy(
             partial.at[peer], arrived.at[me], moment_send, moment_recv,
             device_id={"blk": peer}, device_id_type=MESH,

time: 45.8 us -> 47.2 us (1.031)
  Pallas kernels: 44.2 us -> 45.7 us
    pallas_call x1, Pallas kernels: 44.2 us -> 45.7 us  [on_device(): pl.pallas_call(functools.partial(kernel, n, chunks), out_shape=jax.ShapeD...]
where the time goes in v4:
time: 47.2 us; the launch traced here: 47 us
  Pallas kernels  45.7 us (97%)
  local copies, waits for them, and re-layouts  1.28 us (3%)
    pallas_call x1, Pallas kernels, on_device(): pl.pallas_call(functools.partial(kernel, n, chunks), out_shape=jax.ShapeD...  45.7 us
    unnamed x1, local copies, waits for them, and re-layouts  1.28 us

profile of v4, /device:TPU:0, one launch (start us, length us, event | category | flops | bytes accessed | tf_op | source)
XLA Modules:
  0.0 47.0 jit_solution(3975978239693362245)
XLA Ops:
  0.0 45.7 %shard_map.55 = f32[6,128]{1,0:T(8,128)} custom-call(bf16[6,49152]{1,0:T(8,128)(2,1)} %initial.1, bf16[8,49152]{1,0:T(8,128)(2,1)} %final.1, bf16[3,12,256,256]{3,2,1,0:T(8,128)(2,1)} %dipole.1, s32[12]{0:T(128)} %lengths.1, s32[6,128]{1,0:T(8,128)} %mask.1), custom_call_target="tpu_custom_call" | custom-call | flops 905969664 | bytes 6291456 | tf_op jit(solution)/shard_map/pallas_call | solution.py:232
  45.7 1.3 %copy.7 = f32[6,128]{1,0:T(8,128)} copy(f32[6,128]{1,0:T(8,128)} %shard_map.55) | data formatting | bytes 6144
